TPU v7x, 256 devices: a whole 4x4x8 slice. The times are simulated.
256 devices in a mesh: gz: 8 (over y, z_lo), row: 4 (over z_hi), col: 8 (over x, core).
Axes of the slice: x: 4, y: 4, z: 8 (z_hi: 4, z_lo: 2; z = z_hi * 2 + z_lo), core: 2. Of those that a mesh axis runs over, the one named last changes fastest.
Arguments:
- lower_sub: bfloat16 [8, 2048, 8192], P('gz', 'row'), may hold values from -0.0625 to 0.0625
- upper_sub: bfloat16 [8, 8192, 2048], P('gz', None, 'col'), may hold values from -6 to 6
- block_mask: int32 [8, 16, 16], P('gz', 'row', 'col'), may hold values 0 or 1
- front_base: float32 [2048, 2048], P(('row', 'gz'), 'col'), may hold values from -6 to 6
- pivot_inverse: float32 [2, 256, 256], replicated, may hold values from -0.01 to 0.01
- pivot_order: int32 [2, 256], replicated, may hold values from 0 to 255, each once within a row
Outputs:
- factored: float32 [2048, 2048], P(('row', 'gz'), 'col')
Inputs may be any that keep to these rules, and one draw needn't show every extreme that they name: Each row of pivot_order is a permutation of 0 .. 255.
All inputs are finite; a program needn't handle non-finite values. No bound on the sum of `block_mask` on one device may be relied on, other than what follows from the above.
Results may differ from a plain program's by a relative error of at most 0.0003.
Values sent between devices are 32-bit elements; how exact they have to be, the bound alone decides.
A program may use at most 64 MiB of HBM per device.

v0:
```python
import jax
import jax.numpy as jnp
from jax import lax
from jax.sharding import PartitionSpec as P


def spread_2(block, axis, holder):
    block = jnp.where(lax.axis_index(axis) == holder, block, jnp.zeros_like(block))
    return lax.psum(block, axis)


def on_device(lower_sub, upper_sub, block_mask, front_base, pivot_inverse, pivot_order):
    highest = lax.Precision.HIGHEST
    left_factor = lower_sub[0]
    right_factor = upper_sub[0]
    slab_rows = left_factor.shape[0]
    own_rows, own_cols = front_base.shape
    tiles = block_mask[0].astype(jnp.float32)
    tile_rows = slab_rows // tiles.shape[0]
    tile_cols = own_cols // tiles.shape[1]
    spread = jnp.broadcast_to(
        tiles[:, None, :, None], (tiles.shape[0], tile_rows, tiles.shape[1], tile_cols)
    ).reshape(slab_rows, own_cols)
    summed = lax.psum_scatter(
        jnp.dot(left_factor, right_factor, preferred_element_type=jnp.float32) * spread,
        "gz",
        scatter_dimension=0,
        tiled=True,
    )
    front = front_base + summed
    block_index = lax.axis_index("row") * lax.axis_size("gz") + lax.axis_index("gz")
    row_ids = block_index * own_rows + jnp.arange(own_rows, dtype=jnp.int32)
    col_ids = lax.axis_index("col") * own_cols + jnp.arange(own_cols, dtype=jnp.int32)
    panel_width = pivot_inverse.shape[1]
    for panel in range(pivot_inverse.shape[0]):
        start_row = panel * panel_width
        after_row = start_row + panel_width
        targets = start_row + jnp.arange(panel_width, dtype=jnp.int32)
        placer = (targets[:, None] == row_ids[None, :]).astype(jnp.float32)
        owned = (row_ids >= start_row) & (row_ids < after_row)
        column_rows = lax.all_gather(front, "gz", axis=0, tiled=True)
        pivot_block = spread_2(column_rows[start_row:after_row], "row", 0)
        permuted = jnp.take(pivot_block, pivot_order[panel], axis=0)
        placed = jnp.dot(placer.T, permuted, precision=highest)
        front = jnp.where(owned[:, None], placed, front)
        root_col = start_row // own_cols
        offset = start_row - root_col * own_cols
        panel_cols = front
        beneath = row_ids >= after_row
        lower = jnp.where(
            beneath[:, None], jnp.dot(panel_cols, pivot_inverse[panel], precision=highest), 0.0
        )
        lower = spread_2(lower, "col", root_col)
        is_root = lax.axis_index("col") == root_col
        front = front.at[:, offset : offset + panel_width].set(
            jnp.where(beneath[:, None] & is_root, lower, panel_cols)
        )
        update = jnp.dot(lower, permuted, precision=highest)
        front = front - jnp.where((col_ids >= after_row)[None, :], update, 0.0)
    return front


def solution(mesh):
    placed = (
        P("gz", "row", None),
        P("gz", None, "col"),
        P("gz", "row", "col"),
        P(("row", "gz"), "col"),
        P(),
        P(),
    )
    return jax.shard_map(
        on_device, mesh=mesh, in_specs=placed, out_specs=P(("row", "gz"), "col"), check_vma=False
    )
```

profile of v0, /device:TPU:8, one launch (start us, length us, event | category | flops | bytes accessed | tf_op | source)
XLA Modules:
  0.0 361.3 jit_solution(12610471177662328038)
XLA Ops:
  6.5 0.7 convert_bitcast_fusion
  7.2 0.1 copy.7
  7.3 0.2 broadcast_in_dim.90
  7.5 0.0 copy-start.1
  7.6 7.8 %fusion.3 = f32[512,256]{1,0:T(8,128)} fusion(bf16[1,8192,256]{2,1,0:T(8,128)(2,1)} %param.17, bf16[1,512,8192]{2,1,0:T(8,128)(2,1)} %param.16, f32[64,8,2,128]{3,2,1,0:T(2,128)S(1)} %bitcast.28), kind=kOutput, calls=%fused_computation.5 | convolution fusion | flops 2147614720 | bytes 13631488 | tf_op jit(solution)/shard_map/dot_general | solution.py:25
  15.3 0.0 reduce-scatter.2.cloned.1.call-update
  15.3 0.0 all-reduce.5.cloned.1.call-start
  15.5 41.5 %reduce-scatter.2.cloned.1.call-done = f32[64,256]{1,0:T(8,128)} async-done(((f32[512,256]{1,0:T(8,128)}), f32[64,256]{1,0:T(8,128)}) %reduce-scatter.2.cloned.1.call-update) | async-done | bytes 65552 | tf_op jit(solution)/shard_map/reduce_scatter | solution.py:24
  57.0 0.8 add.81
  57.9 30.0 %all_gather.6 = f32[512,256]{1,0:T(8,128)S(1)} all-gather(f32[64,256]{1,0:T(8,128)S(1)} %add.81), channel_id=1, replica_groups=mesh['gz'=8,'row'=4,'col'=8] {'gz'}, dimensions={0}, use_global_device_ids=true | all-gather | bytes 589824 | tf_op jit(solution)/shard_map/all_gather | solution.py:41
  87.8 0.7 slice_select_fusion.1
  88.5 0.0 all-reduce.5.cloned.1.call-update
  88.6 0.0 all-reduce.7.cloned.1.call-start
  88.6 51.6 %all-reduce.5.cloned.1.call-done = f32[256,256]{1,0:T(8,128)} async-done(((f32[256,256]{1,0:T(8,128)}), f32[256,256]{1,0:T(8,128)}) %all-reduce.5.cloned.1.call-update) | async-done | bytes 262160 | tf_op jit(solution)/shard_map/psum | solution.py:9
  140.2 1.9 gather_fusion
  142.1 0.3 convolution_select_fusion.5
  142.5 0.9 fusion.11
  143.4 0.0 all-reduce.7.cloned.1.call-update
  143.4 0.0 all-reduce.9.cloned.1.call-start
  143.5 62.5 %all-reduce.7.cloned.1.call-done = f32[64,256]{1,0:T(8,128)} async-done(((f32[64,256]{1,0:T(8,128)}), f32[64,256]{1,0:T(8,128)}) %all-reduce.7.cloned.1.call-update) | async-done | bytes 65552 | tf_op jit(solution)/shard_map/psum | solution.py:9
  206.0 1.3 fusion.10
  207.2 28.0 %all_gather.7 = f32[512,256]{1,0:T(8,128)S(1)} all-gather(f32[64,256]{1,0:T(8,128)S(1)} %fusion.10), channel_id=1, replica_groups=mesh['gz'=8,'row'=4,'col'=8] {'gz'}, dimensions={0}, use_global_device_ids=true | all-gather | bytes 589824 | tf_op jit(solution)/shard_map/all_gather | solution.py:41
  235.2 0.7 slice_select_fusion
  235.9 0.0 all-reduce.9.cloned.1.call-update
  235.9 0.0 all-reduce.11.cloned.1.call-start
  236.0 51.1 %all-reduce.9.cloned.1.call-done = f32[256,256]{1,0:T(8,128)} async-done(((f32[256,256]{1,0:T(8,128)}), f32[256,256]{1,0:T(8,128)}) %all-reduce.9.cloned.1.call-update) | async-done | bytes 262160 | tf_op jit(solution)/shard_map/psum | solution.py:9
  287.1 1.9 gather_fusion.1
  289.0 0.4 convolution_select_fusion.2
  289.4 0.9 fusion.9
  290.3 0.0 all-reduce.11.cloned.1.call-update
  290.3 62.6 %all-reduce.11.cloned.1.call-done = f32[64,256]{1,0:T(8,128)} async-done(((f32[64,256]{1,0:T(8,128)}), f32[64,256]{1,0:T(8,128)}) %all-reduce.11.cloned.1.call-update) | async-done | bytes 65552 | tf_op jit(solution)/shard_map/psum | solution.py:9
  352.9 1.9 fusion.8
  (22 shorter events, 0.1 us)
Async XLA Ops:
  6.5 50.5 %reduce-scatter.2.cloned.1.call-start = ((), (), s32[]{:S(2)}) async-start(), calls=%async_computation.1 | async-start | bytes 589824 | tf_op jit(solution)/shard_map/reduce_scatter | solution.py:24
  7.5 8.0 %copy-start.2 = (s32[2,256]{1,0:T(2,128)S(1)}, s32[2,256]{1,0:T(2,128)}, u32[]{:S(2)}) copy-start(s32[2,256]{1,0:T(2,128)} %param.21) | copy-start | bytes 6148
  7.5 49.5 %copy-start.1 = (f32[64,256]{1,0:T(8,128)S(1)}, f32[64,256]{1,0:T(8,128)}, u32[]{:S(2)}) copy-start(f32[64,256]{1,0:T(8,128)} %param.19) | copy-start | bytes 196612
  7.5 134.9 %copy-start = (f32[2,256,256]{2,1,0:T(8,128)S(1)}, f32[2,256,256]{2,1,0:T(8,128)}, u32[]{:S(2)}) copy-start(f32[2,256,256]{2,1,0:T(8,128)} %param.20) | copy-start | bytes 1572868
  15.3 124.9 %all-reduce.5.cloned.1.call-start = ((), (), s32[]{:S(2)}) async-start(), calls=%async_computation.2 | async-start | bytes 524288 | tf_op jit(solution)/shard_map/psum | solution.py:9
  88.6 117.4 %all-reduce.7.cloned.1.call-start = ((), (), s32[]{:S(2)}) async-start(), calls=%async_computation.3 | async-start | bytes 131072 | tf_op jit(solution)/shard_map/psum | solution.py:9
  143.4 143.7 %all-reduce.9.cloned.1.call-start = ((), (), s32[]{:S(2)}) async-start(), calls=%async_computation.4 | async-start | bytes 524288 | tf_op jit(solution)/shard_map/psum | solution.py:9
  235.9 117.0 %all-reduce.11.cloned.1.call-start = ((), (), s32[]{:S(2)}) async-start(), calls=%async_computation.5 | async-start | bytes 131072 | tf_op jit(solution)/shard_map/psum | solution.py:9
Sparse Core Ops, SparseCore 0:
  15.5 41.5 reduce-scatter.1
  88.7 51.4 all-reduce.4
  143.5 62.4 all-reduce.6
  236.1 50.9 all-reduce.8
  290.4 62.4 all-reduce.10
where the time goes:
time: 362 us; the launch traced here: 361 us
  waiting for transfers between devices  269 us (74%)
  blocking collectives  57.9 us (16%)
  matrix products  13.4 us (4%)
  between operations  13.3 us (4%)
  local copies, waits for them, and re-layouts  4.15 us (1%)
    psum x4, waiting for transfers between devices, spread_2(): return lax.psum(block, axis)  228 us
    all_gather x2, blocking collectives, on_device(): column_rows = lax.all_gather(front, 'gz', axis=0, tiled=True)  57.9 us
    reduce_scatter x1, waiting for transfers between devices, on_device(): lax.psum_scatter(jnp.dot(left_factor, right_factor, preferred_element_typ...  41.5 us
    dot_general x1, matrix products, on_device(): jnp.dot(left_factor, right_factor, preferred_element_type=jnp.float32)  7.75 us
  transfers between devices with their start and end apart: 5, of which 5 were waited for; matrix products, arithmetic and copies ran while one was open for 0% of the time, Pallas kernels for 0%

commit v1 on v0

--- a/solution.py
+++ b/solution.py
@@ -2,11 +2,17 @@
 import jax.numpy as jnp
 from jax import lax
 from jax.sharding import PartitionSpec as P
+from jax.lax import all_gather
 
 
 def spread_2(block, axis, holder):
     block = jnp.where(lax.axis_index(axis) == holder, block, jnp.zeros_like(block))
-    return lax.psum(block, axis)
+
+    def scales_touch(frame):
+        block_out = jnp.sum(all_gather(frame, axis_name=axis), axis=0)
+        return block_out
+
+    return scales_touch(block)
 
 
 def on_device(lower_sub, upper_sub, block_mask, front_base, pivot_inverse, pivot_order):

time: 362 us -> 230 us (0.64)
  waiting for transfers between devices: 269 us -> 112 us
  blocking collectives: 57.9 us -> 84.6 us
    psum x4 -> x0, waiting for transfers between devices: 228 us -> none  [spread_2(): return lax.psum(block, axis)]
    all_gather x0 -> x2, waiting for transfers between devices: none -> 69.9 us  [scales_touch(): block_out = jnp.sum(all_gather(frame, axis_name=axis), axis=0)]
    all_gather x0 -> x2, blocking collectives: none -> 26.8 us  [scales_touch(): block_out = jnp.sum(all_gather(frame, axis_name=axis), axis=0)]
  transfers between devices with their start and end apart: 5 -> 3, of which waited for: 5 -> 3; matrix products, arithmetic and copies ran while one was open for 0% -> 0% of each run, Pallas kernels for 0% -> 0%
where the time goes in v1:
time: 230 us; the launch traced here: 228 us
  waiting for transfers between devices  112 us (49%)
  blocking collectives  84.6 us (37%)
  between operations  13.3 us (6%)
  matrix products  10.3 us (4%)
  other arithmetic  5.8 us (3%)
    all_gather x2, waiting for transfers between devices, scales_touch(): block_out = jnp.sum(all_gather(frame, axis_name=axis), axis=0)  69.9 us
    all_gather x2, blocking collectives, on_device(): column_rows = lax.all_gather(front, 'gz', axis=0, tiled=True)  57.8 us
    reduce_scatter x1, waiting for transfers between devices, on_device(): lax.psum_scatter(jnp.dot(left_factor, right_factor, preferred_element_typ...  41.6 us
    all_gather x2, blocking collectives, scales_touch(): block_out = jnp.sum(all_gather(frame, axis_name=axis), axis=0)  26.8 us
    dot_general x1, matrix products, on_device(): jnp.dot(left_factor, right_factor, preferred_element_type=jnp.float32)  7.75 us
  transfers between devices with their start and end apart: 3, of which 3 were waited for; matrix products, arithmetic and copies ran while one was open for 0% of the time, Pallas kernels for 0%

profile of v1, /device:TPU:8, one launch (start us, length us, event | category | flops | bytes accessed | tf_op | source)
XLA Modules:
  0.0 228.0 jit_solution(11984325215547632033)
XLA Ops:
  6.5 0.7 convert_bitcast_fusion
  7.2 0.1 copy.7
  7.3 0.2 broadcast_in_dim.90
  7.5 0.0 copy-start.1
  7.5 0.0 copy-start.2
  7.5 0.0 copy-start
  7.6 7.8 %fusion.3 = f32[512,256]{1,0:T(8,128)} fusion(bf16[1,8192,256]{2,1,0:T(8,128)(2,1)} %param.17, bf16[1,512,8192]{2,1,0:T(8,128)(2,1)} %param.16, f32[64,8,2,128]{3,2,1,0:T(2,128)S(1)} %bitcast.36), kind=kOutput, calls=%fused_computation.5 | convolution fusion | flops 2147614720 | bytes 13631488 | tf_op jit(solution)/shard_map/dot_general | solution.py:31
  15.3 0.0 reduce-scatter.2.cloned.1.call-update
  15.3 0.0 all-gather.7.cloned.1.call-start
  15.4 41.6 %reduce-scatter.2.cloned.1.call-done = f32[64,256]{1,0:T(8,128)} async-done(((f32[512,256]{1,0:T(8,128)}), f32[64,256]{1,0:T(8,128)}) %reduce-scatter.2.cloned.1.call-update) | async-done | bytes 65552 | tf_op jit(solution)/shard_map/reduce_scatter | solution.py:30
  57.0 0.9 add.73
  57.9 30.0 %all_gather.30 = f32[512,256]{1,0:T(8,128)S(1)} all-gather(f32[64,256]{1,0:T(8,128)S(1)} %add.73), channel_id=1, replica_groups=mesh['gz'=8,'row'=4,'col'=8] {'gz'}, dimensions={0}, use_global_device_ids=true | all-gather | bytes 589824 | tf_op jit(solution)/shard_map/all_gather | solution.py:47
  87.8 0.7 slice_select_fusion.1
  88.6 0.0 all-gather.7.cloned.1.call-update
  88.6 0.0 all-gather.9.cloned.1.call-start
  88.8 35.8 %all-gather.7.cloned.1.call-done = f32[1024,256]{1,0:T(8,128)} async-done(((f32[256,256]{1,0:T(8,128)}), f32[1024,256]{1,0:T(8,128)}) %all-gather.7.cloned.1.call-update) | async-done | bytes 1048592 | tf_op jit(solution)/shard_map/all_gather | solution.py:12
  124.6 1.3 reduce_sum.36
  125.9 1.0 gather_fusion
  126.9 0.3 convolution_select_fusion.5
  127.2 0.2 fusion.11
  127.5 13.4 %all-gather.1 = f32[512,256]{1,0:T(8,128)S(1)} all-gather(f32[64,256]{1,0:T(8,128)S(1)} %fusion.11), channel_id=3, replica_groups=mesh['gz'=8,'row'=4,'col'=8] {'col'}, dimensions={0}, use_global_device_ids=true | all-gather | bytes 589824 | tf_op jit(solution)/shard_map/all_gather | solution.py:12
  140.9 0.4 fusion.10
  141.3 27.9 %all_gather.35 = f32[512,256]{1,0:T(8,128)S(1)} all-gather(f32[64,256]{1,0:T(8,128)S(1)} %fusion.10), channel_id=1, replica_groups=mesh['gz'=8,'row'=4,'col'=8] {'gz'}, dimensions={0}, use_global_device_ids=true | all-gather | bytes 589824 | tf_op jit(solution)/shard_map/all_gather | solution.py:47
  169.1 0.7 slice_select_fusion
  169.9 0.0 all-gather.9.cloned.1.call-update
  170.0 34.1 %all-gather.9.cloned.1.call-done = f32[1024,256]{1,0:T(8,128)} async-done(((f32[256,256]{1,0:T(8,128)}), f32[1024,256]{1,0:T(8,128)}) %all-gather.9.cloned.1.call-update) | async-done | bytes 1048592 | tf_op jit(solution)/shard_map/all_gather | solution.py:12
  204.1 1.3 reduce_sum.38
  205.4 1.0 gather_fusion.1
  206.4 0.4 convolution_select_fusion.2
  206.8 0.2 fusion.9
  207.0 13.4 %all-gather.3 = f32[512,256]{1,0:T(8,128)S(1)} all-gather(f32[64,256]{1,0:T(8,128)S(1)} %fusion.9), channel_id=5, replica_groups=mesh['gz'=8,'row'=4,'col'=8] {'col'}, dimensions={0}, use_global_device_ids=true | all-gather | bytes 589824 | tf_op jit(solution)/shard_map/all_gather | solution.py:12
  220.5 1.0 fusion.8
  (21 shorter events, 0.2 us)
Async XLA Ops:
  6.5 50.5 %reduce-scatter.2.cloned.1.call-start = ((), (), s32[]{:S(2)}) async-start(), calls=%async_computation.1 | async-start | bytes 589824 | tf_op jit(solution)/shard_map/reduce_scatter | solution.py:30
  7.5 49.5 %copy-start.1 = (f32[64,256]{1,0:T(8,128)S(1)}, f32[64,256]{1,0:T(8,128)}, u32[]{:S(2)}) copy-start(f32[64,256]{1,0:T(8,128)} %param.19) | copy-start | bytes 196612
  7.5 81.2 %copy-start.2 = (s32[2,256]{1,0:T(2,128)S(1)}, s32[2,256]{1,0:T(2,128)}, u32[]{:S(2)}) copy-start(s32[2,256]{1,0:T(2,128)} %param.21) | copy-start | bytes 6148
  7.5 119.6 %copy-start = (f32[2,256,256]{2,1,0:T(8,128)S(1)}, f32[2,256,256]{2,1,0:T(8,128)}, u32[]{:S(2)}) copy-start(f32[2,256,256]{2,1,0:T(8,128)} %param.20) | copy-start | bytes 1572868
  15.3 109.2 %all-gather.7.cloned.1.call-start = ((), (), s32[]{:S(2)}) async-start(), calls=%async_computation.2 | async-start | bytes 1310720 | tf_op jit(solution)/shard_map/all_gather | solution.py:12
  88.6 115.5 %all-gather.9.cloned.1.call-start = ((), (), s32[]{:S(2)}) async-start(), calls=%async_computation.3 | async-start | bytes 1310720 | tf_op jit(solution)/shard_map/all_gather | solution.py:12
Sparse Core Ops, SparseCore 0:
  15.5 41.5 reduce-scatter.1
  88.7 35.7 all-gather.6
  170.0 34.0 all-gather.8

commit v2 on v0

--- a/solution.py
+++ b/solution.py
@@ -2,6 +2,7 @@
 import jax.numpy as jnp
 from jax import lax
 from jax.sharding import PartitionSpec as P
+from jax.lax import all_to_all, psum
 
 
 def spread_2(block, axis, holder):
@@ -38,7 +39,10 @@
         targets = start_row + jnp.arange(panel_width, dtype=jnp.int32)
         placer = (targets[:, None] == row_ids[None, :]).astype(jnp.float32)
         owned = (row_ids >= start_row) & (row_ids < after_row)
-        column_rows = lax.all_gather(front, "gz", axis=0, tiled=True)
+        b_next = tuple((front for _ in range(psum(1, "gz"))))
+        taken_in = jnp.stack(b_next)
+        v_now = all_to_all(taken_in, "gz", 0, 0)
+        column_rows = jnp.concatenate(v_now, 0)
         pivot_block = spread_2(column_rows[start_row:after_row], "row", 0)
         permuted = jnp.take(pivot_block, pivot_order[panel], axis=0)
         placed = jnp.dot(placer.T, permuted, precision=highest)

time: 362 us -> 330 us (0.912)
  blocking collectives: 57.9 us -> 0 us
  waiting for transfers between devices: 269 us -> 281 us
  starting transfers between devices: 0.17 us -> 12.1 us
    all_gather x2 -> x0, blocking collectives: 57.9 us -> none  [on_device(): column_rows = lax.all_gather(front, 'gz', axis=0, tiled=True)]
    all_to_all x0 -> x2, waiting for transfers between devices: none -> 13.5 us  [on_device(): v_now = all_to_all(taken_in, 'gz', 0, 0)]
    all_to_all x0 -> x2, starting transfers between devices: none -> 12 us  [on_device(): v_now = all_to_all(taken_in, 'gz', 0, 0)]
  transfers between devices with their start and end apart: 5 -> 7, of which waited for: 5 -> 7; matrix products, arithmetic and copies ran while one was open for 0% -> 0% of each run, Pallas kernels for 0% -> 0%
where the time goes in v2:
time: 330 us; the launch traced here: 329 us
  waiting for transfers between devices  281 us (85%)
  matrix products  13.4 us (4%)
  between operations  13.3 us (4%)
  starting transfers between devices  12.1 us (4%)
  local copies, waits for them, and re-layouts  5.84 us (2%)
    psum x4, waiting for transfers between devices, spread_2(): return lax.psum(block, axis)  226 us
    reduce_scatter x1, waiting for transfers between devices, on_device(): lax.psum_scatter(jnp.dot(left_factor, right_factor, preferred_element_typ...  41.7 us
    all_to_all x2, waiting for transfers between devices, on_device(): v_now = all_to_all(taken_in, 'gz', 0, 0)  13.5 us
    all_to_all x2, starting transfers between devices, on_device(): v_now = all_to_all(taken_in, 'gz', 0, 0)  12 us
    dot_general x1, matrix products, on_device(): jnp.dot(left_factor, right_factor, preferred_element_type=jnp.float32)  7.76 us
  transfers between devices with their start and end apart: 7, of which 7 were waited for; matrix products, arithmetic and copies ran while one was open for 0% of the time, Pallas kernels for 0%

profile of v2, /device:TPU:8, one launch (start us, length us, event | category | flops | bytes accessed | tf_op | source)
XLA Modules:
  0.0 329.1 jit_solution(10025001320919555267)
XLA Ops:
  6.5 0.7 convert_bitcast_fusion
  7.2 0.1 copy.7
  7.3 0.2 broadcast_in_dim.90
  7.6 7.8 %fusion.3 = f32[512,256]{1,0:T(8,128)} fusion(bf16[1,8192,256]{2,1,0:T(8,128)(2,1)} %param.17, bf16[1,512,8192]{2,1,0:T(8,128)(2,1)} %param.16, f32[64,8,2,128]{3,2,1,0:T(2,128)S(1)} %bitcast.32), kind=kOutput, calls=%fused_computation.5 | convolution fusion | flops 2147614720 | bytes 13631488 | tf_op jit(solution)/shard_map/dot_general | solution.py:26
  15.3 0.0 reduce-scatter.2.cloned.1.call-update
  15.3 41.7 %reduce-scatter.2.cloned.1.call-done = f32[64,256]{1,0:T(8,128)} async-done(((f32[512,256]{1,0:T(8,128)}), f32[64,256]{1,0:T(8,128)}) %reduce-scatter.2.cloned.1.call-update) | async-done | bytes 65552 | tf_op jit(solution)/shard_map/reduce_scatter | solution.py:25
  57.1 0.8 add.81
  57.9 0.8 stack.4
  58.7 6.1 %all-to-all-start = ((f32[8,64,256]{2,1,0:T(8,128)}), f32[8,64,256]{2,1,0:T(8,128)S(1)}, u32[]{:S(2)}, u32[]{:S(2)}) async-start(f32[8,64,256]{2,1,0:T(8,128)} %stack.4), calls=%async_computation.1 | async-start | bytes 1048576 | tf_op jit(solution)/shard_map/all_to_all | solution.py:44
  65.0 6.8 %all-to-all-done = f32[8,64,256]{2,1,0:T(8,128)S(1)} async-done(((f32[8,64,256]{2,1,0:T(8,128)}), f32[8,64,256]{2,1,0:T(8,128)S(1)}, u32[]{:S(2)}, u32[]{:S(2)}) %all-to-all-start) | async-done | bytes 524320 | tf_op jit(solution)/shard_map/all_to_all | solution.py:44
  71.7 0.7 slice_select_fusion.1
  72.5 0.0 all-reduce.5.cloned.1.call-update
  72.5 0.0 all-reduce.7.cloned.1.call-start
  72.6 50.6 %all-reduce.5.cloned.1.call-done = f32[256,256]{1,0:T(8,128)} async-done(((f32[256,256]{1,0:T(8,128)}), f32[256,256]{1,0:T(8,128)}) %all-reduce.5.cloned.1.call-update) | async-done | bytes 262160 | tf_op jit(solution)/shard_map/psum | solution.py:10
  123.2 1.9 gather_fusion
  125.1 0.3 convolution_select_fusion.5
  125.4 0.9 fusion.11
  126.3 0.0 all-reduce.7.cloned.1.call-update
  126.4 62.6 %all-reduce.7.cloned.1.call-done = f32[64,256]{1,0:T(8,128)} async-done(((f32[64,256]{1,0:T(8,128)}), f32[64,256]{1,0:T(8,128)}) %all-reduce.7.cloned.1.call-update) | async-done | bytes 65552 | tf_op jit(solution)/shard_map/psum | solution.py:10
  189.0 1.3 fusion.10
  190.2 0.8 stack.5
  191.1 5.8 %all-to-all-start.1 = ((f32[8,64,256]{2,1,0:T(8,128)}), f32[8,64,256]{2,1,0:T(8,128)S(1)}, u32[]{:S(2)}, u32[]{:S(2)}) async-start(f32[8,64,256]{2,1,0:T(8,128)} %stack.5), calls=%async_computation.2 | async-start | bytes 1048576 | tf_op jit(solution)/shard_map/all_to_all | solution.py:44
  197.0 6.8 %all-to-all-done.1 = f32[8,64,256]{2,1,0:T(8,128)S(1)} async-done(((f32[8,64,256]{2,1,0:T(8,128)}), f32[8,64,256]{2,1,0:T(8,128)S(1)}, u32[]{:S(2)}, u32[]{:S(2)}) %all-to-all-start.1) | async-done | bytes 524320 | tf_op jit(solution)/shard_map/all_to_all | solution.py:44
  203.7 0.7 slice_select_fusion
  204.5 0.0 all-reduce.9.cloned.1.call-update
  204.5 0.0 all-reduce.11.cloned.1.call-start
  204.6 50.3 %all-reduce.9.cloned.1.call-done = f32[256,256]{1,0:T(8,128)} async-done(((f32[256,256]{1,0:T(8,128)}), f32[256,256]{1,0:T(8,128)}) %all-reduce.9.cloned.1.call-update) | async-done | bytes 262160 | tf_op jit(solution)/shard_map/psum | solution.py:10
  254.9 1.9 gather_fusion.1
  256.8 0.4 convolution_select_fusion.2
  257.2 0.9 fusion.9
  258.1 62.6 %all-reduce.11.cloned.1.call-done = f32[64,256]{1,0:T(8,128)} async-done(((f32[64,256]{1,0:T(8,128)}), f32[64,256]{1,0:T(8,128)}) %all-reduce.11.cloned.1.call-update) | async-done | bytes 65552 | tf_op jit(solution)/shard_map/psum | solution.py:10
  320.7 1.9 fusion.8
  (26 shorter events, 0.1 us)
Async XLA Ops:
  6.5 50.5 %reduce-scatter.2.cloned.1.call-start = ((), (), s32[]{:S(2)}) async-start(), calls=%async_computation.3 | async-start | bytes 589824 | tf_op jit(solution)/shard_map/reduce_scatter | solution.py:25
  7.5 49.5 %copy-start.1 = (f32[64,256]{1,0:T(8,128)S(1)}, f32[64,256]{1,0:T(8,128)}, u32[]{:S(2)}) copy-start(f32[64,256]{1,0:T(8,128)} %param.19) | copy-start | bytes 196612
  7.5 57.4 %copy-start.2 = (s32[2,256]{1,0:T(2,128)S(1)}, s32[2,256]{1,0:T(2,128)}, u32[]{:S(2)}) copy-start(s32[2,256]{1,0:T(2,128)} %param.21) | copy-start | bytes 6148
  7.5 117.9 %copy-start = (f32[2,256,256]{2,1,0:T(8,128)S(1)}, f32[2,256,256]{2,1,0:T(8,128)}, u32[]{:S(2)}) copy-start(f32[2,256,256]{2,1,0:T(8,128)} %param.20) | copy-start | bytes 1572868
  58.7 13.0 %all-to-all-start = ((f32[8,64,256]{2,1,0:T(8,128)}), f32[8,64,256]{2,1,0:T(8,128)S(1)}, u32[]{:S(2)}, u32[]{:S(2)}) async-start(f32[8,64,256]{2,1,0:T(8,128)} %stack.4), calls=%async_computation.1 | async-start | bytes 1048576 | tf_op jit(solution)/shard_map/all_to_all | solution.py:44
  64.9 58.3 %all-reduce.5.cloned.1.call-start = ((), (), s32[]{:S(2)}) async-start(), calls=%async_computation.4 | async-start | bytes 524288 | tf_op jit(solution)/shard_map/psum | solution.py:10
  72.5 116.5 %all-reduce.7.cloned.1.call-start = ((), (), s32[]{:S(2)}) async-start(), calls=%async_computation.5 | async-start | bytes 131072 | tf_op jit(solution)/shard_map/psum | solution.py:10
  191.1 12.6 %all-to-all-start.1 = ((f32[8,64,256]{2,1,0:T(8,128)}), f32[8,64,256]{2,1,0:T(8,128)S(1)}, u32[]{:S(2)}, u32[]{:S(2)}) async-start(f32[8,64,256]{2,1,0:T(8,128)} %stack.5), calls=%async_computation.2 | async-start | bytes 1048576 | tf_op jit(solution)/shard_map/all_to_all | solution.py:44
  196.9 58.0 %all-reduce.9.cloned.1.call-start = ((), (), s32[]{:S(2)}) async-start(), calls=%async_computation.6 | async-start | bytes 524288 | tf_op jit(solution)/shard_map/psum | solution.py:10
  204.5 116.2 %all-reduce.11.cloned.1.call-start = ((), (), s32[]{:S(2)}) async-start(), calls=%async_computation.7 | async-start | bytes 131072 | tf_op jit(solution)/shard_map/psum | solution.py:10
Sparse Core Ops, SparseCore 0:
  15.5 41.5 reduce-scatter.1
  72.6 50.5 all-reduce.4
  126.5 62.4 all-reduce.6
  204.6 50.2 all-reduce.8
  258.2 62.4 all-reduce.10
